TPU v7x, 32 devices: a whole 2x2x4 slice. The times are simulated.
32 devices in a mesh: section: 2 (over core), dp: 16 (over z, y, x).
Axes of the slice: x: 2, y: 2, z: 4, core: 2. Of those that a mesh axis runs over, the one named last changes fastest.
Arguments:
- tokens: bfloat16 [2, 16, 256, 768], P(None, 'dp'), may hold values from -6 to 6
- order: int32 [2, 16, 1024], P(None, 'dp'), may hold values from 0 to 1023, each once within a row
- sensor: int32 [2, 16], P(None, 'dp'), may hold values from 0 to 3
- cotangent: bfloat16 [2, 16, 1024, 512], P(None, 'dp'), may hold values from -6 to 6
- enc_norm: bfloat16 [4, 768], replicated, may hold values from 0.099609375 to 1.8984375
- enc_qkv: bfloat16 [768, 2304], replicated, may hold values from -0.21875 to 0.21875
- enc_out: bfloat16 [768, 768], replicated, may hold values from -0.875 to 0.875
- enc_bias: bfloat16 [2, 768], replicated, may hold values from -3 to 3
- enc_up: bfloat16 [768, 3072], replicated, may hold values from -0.21875 to 0.21875
- enc_up_bias: bfloat16 [3072], replicated, may hold values from -3 to 3
- enc_down: bfloat16 [3072, 768], replicated, may hold values from -0.109375 to 0.109375
- sensor_table: bfloat16 [4, 768], replicated, may hold values from -3 to 3
- dec_embed: bfloat16 [768, 512], replicated, may hold values from -0.21875 to 0.21875
- dec_norm: bfloat16 [4, 512], replicated, may hold values from 0.099609375 to 1.8984375
- dec_qkv: bfloat16 [512, 768], replicated, may hold values from -0.25 to 0.25
- dec_out: bfloat16 [256, 512], replicated, may hold values from -1.5 to 1.5
- dec_bias: bfloat16 [4, 512], replicated, may hold values from -3 to 3
- dec_up: bfloat16 [512, 2048], replicated, may hold values from -0.25 to 0.25
- dec_up_bias: bfloat16 [2048], replicated, may hold values from -3 to 3
- dec_down: bfloat16 [2048, 512], replicated, may hold values from -0.125 to 0.125
- dec_pos: bfloat16 [1024, 512], replicated, may hold values from -5 to 5
Outputs:
- decoded: float32 [2, 16, 1024, 512], P('section', 'dp')
- input_grad: float32 [2, 16, 256, 768], P('section', 'dp')
- grad_enc_norm: float32 [4, 768], P('section', 'dp')
- grad_enc_qkv: float32 [768, 2304], P('dp', 'section')
- grad_enc_out: float32 [768, 768], P('dp', 'section')
- grad_enc_bias: float32 [2, 768], P('section', 'dp')
- grad_enc_up: float32 [768, 3072], P('dp', 'section')
- grad_enc_up_bias: float32 [3072], P(('section', 'dp'))
- grad_enc_down: float32 [3072, 768], P('dp', 'section')
- grad_sensor_table: float32 [4, 768], P('section', 'dp')
- grad_dec_embed: float32 [768, 512], P('dp', 'section')
- grad_dec_norm: float32 [4, 512], P('section', 'dp')
- grad_dec_qkv: float32 [512, 768], P('dp', 'section')
- grad_dec_out: float32 [256, 512], P('dp', 'section')
- grad_dec_bias: float32 [4, 512], P('section', 'dp')
- grad_dec_up: float32 [512, 2048], P('dp', 'section')
- grad_dec_up_bias: float32 [2048], P(('section', 'dp'))
- grad_dec_down: float32 [2048, 512], P('dp', 'section')
- grad_dec_pos: float32 [1024, 512], P('section', 'dp')
Inputs may be any that keep to these rules, and one draw needn't show every extreme that they name: `order`: each image's row is a permutation of the 1024 patch positions; its first 256 entries are the visible patches, the rest are masked.
All inputs are finite; a program needn't handle non-finite values.
Results may differ from a plain program's by a relative error of at most 0.015.
Values may be sent and summed in bfloat16 or wider, within the bound.
A program may use at most 256 MiB of HBM per device.

v0:
```python
import heapq
import math
from functools import partial

import jax
import jax.numpy as jnp
from jax import lax
from jax.experimental import pallas as pl
from jax.experimental.pallas import tpu as pltpu
from jax.sharding import PartitionSpec as P

HEAD_DIM = 64
MESH = pl.DeviceIdType.MESH
SMALL_ROWS = 32


def layer_norm(hidden, scales, shifts):
    center = hidden - jnp.mean(hidden, axis=-1, keepdims=True)
    spread = jnp.mean(center * center, axis=-1, keepdims=True)
    return center * lax.rsqrt(spread + 1e-05) * scales + shifts


def matmul(left_side, right_side):
    return jnp.dot(left_side, right_side, preferred_element_type=jnp.float32)


def row_contract(left_side, right_side):
    return lax.dot_general(
        left_side, right_side, (((0,), (0,)), ((), ())), preferred_element_type=jnp.float32
    )


def col_contract(left_side, right_side):
    return lax.dot_general(
        left_side, right_side, (((1,), (1,)), ((), ())), preferred_element_type=jnp.float32
    )


def gelu_exact(values):
    return jax.nn.gelu(values, approximate=False)


def block_forward(hidden, weights):
    norms, qkv_w, out_w, biases, up_w, up_bias, down_w = weights
    batch_size, length, feature_width = hidden.shape
    row_count = batch_size * length
    head_count = qkv_w.shape[1] // (3 * HEAD_DIM)
    inner_width = head_count * HEAD_DIM
    norm_rows = norms.astype(jnp.float32)
    bias_rows = biases.astype(jnp.float32)
    normed = (
        layer_norm(hidden, norm_rows[0], norm_rows[1])
        .astype(jnp.bfloat16)
        .reshape(row_count, feature_width)
    )
    packed = (
        matmul(normed, qkv_w)
        .astype(jnp.bfloat16)
        .reshape(batch_size, length, 3, head_count, HEAD_DIM)
    )
    queries = packed[:, :, 0]
    keys_all = packed[:, :, 1]
    values_all = packed[:, :, 2]
    scores = jnp.einsum(
        "bqhd,bkhd->bhqk", queries, keys_all, preferred_element_type=jnp.float32
    ) * HEAD_DIM ** (-0.5)
    row_peak = jnp.max(scores, axis=-1, keepdims=True)
    logsum = row_peak + jnp.log(jnp.sum(jnp.exp(scores - row_peak), axis=-1, keepdims=True))
    probability = jnp.exp(scores - logsum).astype(jnp.bfloat16)
    attended = jnp.einsum(
        "bhqk,bkhd->bqhd", probability, values_all, preferred_element_type=jnp.float32
    )
    attended = attended.astype(jnp.bfloat16).reshape(row_count, inner_width)
    middle = hidden + (matmul(attended, out_w) + bias_rows[0]).reshape(
        batch_size, length, feature_width
    )
    second = (
        layer_norm(middle, norm_rows[2], norm_rows[3])
        .astype(jnp.bfloat16)
        .reshape(row_count, feature_width)
    )
    lifted = matmul(second, up_w) + up_bias.astype(jnp.float32)
    active = gelu_exact(lifted).astype(jnp.bfloat16)
    output = middle + (matmul(active, down_w) + bias_rows[1]).reshape(
        batch_size, length, feature_width
    )
    stored = (hidden, normed, packed, logsum, attended, middle, second, lifted, active)
    return (output, stored)


def block_backward(stored, upstream, weights):
    norms, qkv_w, out_w, biases, up_w, up_bias, down_w = weights
    hidden, normed, packed, logsum, attended, middle, second, lifted, active = stored
    batch_size, length, feature_width = hidden.shape
    row_count = batch_size * length
    head_count = qkv_w.shape[1] // (3 * HEAD_DIM)
    inner_width = head_count * HEAD_DIM
    score_scale = HEAD_DIM ** (-0.5)
    norm_rows = norms.astype(jnp.float32)
    branch_grad = upstream.reshape(row_count, feature_width).astype(jnp.bfloat16)
    grad_down = row_contract(active, branch_grad)
    grad_bias_down = jnp.sum(branch_grad.astype(jnp.float32), axis=0)
    grad_active = col_contract(branch_grad, down_w)
    grad_lifted = jax.vjp(gelu_exact, lifted)[1](grad_active)[0].astype(jnp.bfloat16)
    grad_up = row_contract(second, grad_lifted)
    grad_up_bias = jnp.sum(grad_lifted.astype(jnp.float32), axis=0)
    grad_second = col_contract(grad_lifted, up_w).reshape(batch_size, length, feature_width)
    grad_middle, grad_scale_two, grad_shift_two = jax.vjp(
        layer_norm, middle, norm_rows[2], norm_rows[3]
    )[1](grad_second)
    grad_middle = upstream + grad_middle
    attn_grad = grad_middle.reshape(row_count, feature_width).astype(jnp.bfloat16)
    grad_out = row_contract(attended, attn_grad)
    grad_bias_out = jnp.sum(attn_grad.astype(jnp.float32), axis=0)
    grad_attended = (
        col_contract(attn_grad, out_w)
        .astype(jnp.bfloat16)
        .reshape(batch_size, length, head_count, HEAD_DIM)
    )
    queries = packed[:, :, 0]
    keys_all = packed[:, :, 1]
    values_all = packed[:, :, 2]
    scores = (
        jnp.einsum("bqhd,bkhd->bhqk", queries, keys_all, preferred_element_type=jnp.float32)
        * score_scale
    )
    probability = jnp.exp(scores - logsum)
    grad_probs = jnp.einsum(
        "bqhd,bkhd->bhqk", grad_attended, values_all, preferred_element_type=jnp.float32
    )
    grad_values = jnp.einsum(
        "bhqk,bqhd->bkhd",
        probability.astype(jnp.bfloat16),
        grad_attended,
        preferred_element_type=jnp.float32,
    )
    row_dots = jnp.sum(grad_probs * probability, axis=-1, keepdims=True)
    grad_scores = (probability * (grad_probs - row_dots)).astype(jnp.bfloat16)
    grad_queries = (
        jnp.einsum("bhqk,bkhd->bqhd", grad_scores, keys_all, preferred_element_type=jnp.float32)
        * score_scale
    )
    grad_keys = (
        jnp.einsum("bhqk,bqhd->bkhd", grad_scores, queries, preferred_element_type=jnp.float32)
        * score_scale
    )
    grad_packed = (
        jnp.stack([grad_queries, grad_keys, grad_values], axis=2)
        .astype(jnp.bfloat16)
        .reshape(row_count, 3 * inner_width)
    )
    grad_qkv = row_contract(normed, grad_packed)
    grad_normed = col_contract(grad_packed, qkv_w).reshape(batch_size, length, feature_width)
    grad_hidden, grad_scale_one, grad_shift_one = jax.vjp(
        layer_norm, hidden, norm_rows[0], norm_rows[1]
    )[1](grad_normed)
    grad_hidden = grad_middle + grad_hidden
    grad_norms = jnp.stack([grad_scale_one, grad_shift_one, grad_scale_two, grad_shift_two])
    grad_biases = jnp.stack([grad_bias_out, grad_bias_down])
    return (
        grad_hidden,
        (grad_norms, grad_qkv, grad_out, grad_biases, grad_up, grad_up_bias, grad_down),
    )


def encode(tokens_part, sensor_part, enc_w):
    table = enc_w[7].astype(jnp.float32)
    picks = (sensor_part[:, None] == jnp.arange(table.shape[0])[None, :]).astype(jnp.float32)
    start = (
        tokens_part.astype(jnp.float32)
        + jnp.sum(picks[:, :, None] * table[None], axis=1)[:, None, :]
    )
    output, stored = block_forward(start, enc_w[:7])
    return (output.astype(jnp.bfloat16), stored, picks)


def encode_back(stored, picks, returned, enc_w):
    grad_input, grads = block_backward(stored, returned.astype(jnp.float32), enc_w[:7])
    grad_table = jnp.sum(picks[:, :, None] * jnp.sum(grad_input, axis=1)[:, None, :], axis=0)
    return (grad_input, grads + (grad_table,))


def decode(arrived, place, cotangent_part, dec_w):
    dec_embed, dec_norm, dec_qkv, dec_out, dec_bias, dec_up, dec_up_bias, dec_down, dec_pos = dec_w
    batch_size, visible, model_width = arrived.shape
    patches = place.shape[1]
    bias_rows = dec_bias.astype(jnp.float32)
    flat_rows = arrived.reshape(batch_size * visible, model_width)
    embedded = (matmul(flat_rows, dec_embed) + bias_rows[0]).reshape(
        batch_size, visible, bias_rows.shape[1]
    )
    filler = jnp.broadcast_to(bias_rows[3], (batch_size, patches - visible, bias_rows.shape[1]))
    sequence = jnp.concatenate([embedded, filler], axis=1)
    image_rows = jnp.arange(batch_size)[:, None]
    placed = jnp.zeros_like(sequence).at[image_rows, place].set(sequence) + dec_pos.astype(
        jnp.float32
    )
    block_w = (dec_norm, dec_qkv, dec_out, bias_rows[1:3], dec_up, dec_up_bias, dec_down)
    output, stored = block_forward(placed, block_w)
    grad_placed, grads = block_backward(stored, cotangent_part.astype(jnp.float32), block_w)
    grad_pos = jnp.sum(grad_placed, axis=0)
    grad_sequence = jnp.take_along_axis(grad_placed, place[:, :, None], axis=1)
    grad_embedded = (
        grad_sequence[:, :visible]
        .reshape(batch_size * visible, bias_rows.shape[1])
        .astype(jnp.bfloat16)
    )
    grad_filler = jnp.sum(grad_sequence[:, visible:], axis=(0, 1))
    grad_embed = row_contract(flat_rows, grad_embedded)
    grad_bias_embed = jnp.sum(grad_embedded.astype(jnp.float32), axis=0)
    returned = (
        col_contract(grad_embedded, dec_embed)
        .astype(jnp.bfloat16)
        .reshape(batch_size, visible, model_width)
    )
    grad_norms, grad_qkv, grad_out, grad_biases, grad_up, grad_up_bias, grad_down = grads
    grad_bias = jnp.stack([grad_bias_embed, grad_biases[0], grad_biases[1], grad_filler])
    return (
        output,
        returned,
        (
            grad_embed,
            grad_norms,
            grad_qkv,
            grad_out,
            grad_bias,
            grad_up,
            grad_up_bias,
            grad_down,
            grad_pos,
        ),
    )


CORE = -1


def partner_of(stage):
    section, data = lax.axis_index("section"), lax.axis_index("dp")
    if stage == CORE:
        return (1 - section, data)
    weight = 2**stage
    bit = lax.rem(data // weight, 2)
    return (section, data + weight * (1 - 2 * bit))


def bit_of(stage):
    if stage == CORE:
        return lax.axis_index("section")
    return lax.rem(lax.axis_index("dp") // 2**stage, 2)


def greet(bits):
    barrier = pltpu.get_barrier_semaphore()
    for stage in [CORE] + list(range(bits)):
        pl.semaphore_signal(barrier, inc=1, device_id=partner_of(stage), device_id_type=MESH)


def greeted(bits):
    pl.semaphore_wait(pltpu.get_barrier_semaphore(), bits + 1)


class Chunk:
    def __init__(self, source, rows, cols, stages, lands, send_sems, recv_sems, result):
        self.source, self.rows, self.cols, self.stages = source, rows, cols, stages
        self.lands, self.send_sems, self.recv_sems = lands, send_sems, recv_sems
        self.result = result
        self.dims = list(range(len(stages) - 2, -1, -1))

    def halves(self, step):
        stage = self.stages[step]
        bit = bit_of(stage)
        if stage == CORE:
            width = self.source.shape[-1] // 2
            start, extent = self.cols

            def part(side):
                offset = pl.multiple_of(side * width + start, 128)
                return self.source.at[
                    (slice(None),) * len(self.dims)
                    + (pl.ds(self.rows[0], self.rows[1]), pl.ds(offset, extent))
                ]

            return part(1 - bit), part(bit)
        held = self.lands[step - 1]
        left = [item for item in self.dims if item not in self.stages[1:step]]
        place = left.index(stage)

        def part(side):
            return held.at[(slice(None),) * place + (side,)]

        return part(1 - bit), part(bit)

    def copy(self, step):
        return pltpu.make_async_remote_copy(
            src_ref=self.halves(step)[0],
            dst_ref=self.lands[step],
            send_sem=self.send_sems.at[step],
            recv_sem=self.recv_sems.at[step],
            device_id=partner_of(self.stages[step]),
            device_id_type=MESH,
        )

    def start(self, step):
        self.copy(step).start()

    def finish(self, step):
        self.copy(step).wait_recv()
        kept, land = self.halves(step)[1], self.lands[step]
        if len(land.shape) > 2:
            land[...] = land[...] + kept[...]
            self.start(step + 1)
        else:
            self.result[pl.ds(*self.rows), pl.ds(*self.cols)] = land[...].astype(
                jnp.float32
            ) + kept[...].astype(jnp.float32)

    def close(self):
        for step in range(len(self.stages)):
            self.copy(step).wait_send()


class Whole:
    def __init__(self, source, bits, lands, send_sems, recv_sems, result):
        self.source, self.lands, self.send_sems, self.recv_sems = source, lands, send_sems, recv_sems
        self.stages = [CORE] + list(range(bits))
        self.result = result

    def held(self, step):
        return self.source if step == 0 else self.lands.at[step - 1]

    def copy(self, step):
        return pltpu.make_async_remote_copy(
            src_ref=self.held(step),
            dst_ref=self.lands.at[step],
            send_sem=self.send_sems.at[step],
            recv_sem=self.recv_sems.at[step],
            device_id=partner_of(self.stages[step]),
            device_id_type=MESH,
        )

    def start(self, step):
        self.copy(step).start()

    def finish(self, step):
        self.copy(step).wait_recv()
        total = self.lands[step] + self.held(step)[...]
        if step == len(self.stages) - 1:
            self.result[...] = total
        else:
            self.lands[step] = total
            self.start(step + 1)

    def close(self):
        for step in range(len(self.stages)):
            self.copy(step).wait_send()


class Flow:
    def __init__(self, steps, lag):
        self.steps, self.lag = steps, lag
        self.waves, self.tick_now = [], 0

    def add(self, chunks):
        for chunk in chunks:
            chunk.start(0)
        self.waves.append([chunks, 0, self.tick_now + 1])

    def tick(self):
        self.tick_now += 1
        for wave in self.waves:
            chunks, step, due = wave
            if step < self.steps and due <= self.tick_now:
                for chunk in chunks:
                    chunk.finish(step)
                wave[1], wave[2] = step + 1, self.tick_now + self.lag

    def drain(self):
        while any(wave[1] < self.steps for wave in self.waves):
            self.tick()
        for wave in self.waves:
            for chunk in wave[0]:
                chunk.close()


def orders_of(bits):
    near = bits // 3
    x, y, z = list(range(near)), list(range(near, 2 * near)), list(range(2 * near, bits))
    return [
        ([CORE] + x + y + z, (0.5, 0.25, 0.1875)),
        ([CORE] + y + x + z, (0.25, 0.5, 0.1875)),
        ([CORE] + z + x + y, (0.125, 0.0625, 0.75)),
        ([CORE] + z + y + x, (0.0625, 0.125, 0.75)),
    ]


def wave_plan(rows, width, orders, loads):
    by_rows = rows >= 128
    unit = 16 if by_rows else 128
    strips = (rows if by_rows else width) // unit
    count = 2 if rows * width > 48 * 1024 else 1
    waves = []
    for item in range(count):
        low, high = strips * item // count, strips * (item + 1) // count
        taken = []
        for _ in range(low, high):
            totals = [
                [old + new * rows * width / strips for old, new in zip(loads, cost)]
                for _, cost in orders
            ]
            best = min(range(len(orders)), key=lambda which: max(totals[which]))
            loads[:] = totals[best]
            taken.append(best)
        wave = []
        for which in sorted(set(taken)):
            extent = taken.count(which)
            cut = (low * unit, extent * unit)
            low += extent
            wave.append((cut, (0, width), which) if by_rows else ((0, rows), cut, which))
        waves.append(wave)
    return waves


F32, BF16 = jnp.float32, jnp.bfloat16
BLOCK = 256
LANES = 256


def dot(left, right):
    return jnp.dot(left, right, preferred_element_type=F32)


def dot_nt(left, right):
    return lax.dot_general(left, right, (((1,), (1,)), ((), ())), preferred_element_type=F32)


def head_of_lane(rows, width=LANES):
    return lax.broadcasted_iota(jnp.int32, (rows, width), 1) // HEAD_DIM


def only_head(rows, head):
    lane = lax.broadcasted_iota(jnp.int32, rows.shape, 1)
    keep = (lane >= head * HEAD_DIM) & (lane < (head + 1) * HEAD_DIM)
    return jnp.where(keep, rows, jnp.zeros_like(rows))


def normalize(values):
    center = values - jnp.mean(values, axis=-1, keepdims=True)
    inverse = lax.rsqrt(jnp.mean(center * center, axis=-1, keepdims=True) + 1e-05)
    return center * inverse, inverse


def gelu_pair(values):
    area = 0.5 + 0.5 * lax.erf(values * 0.7071067811865476)
    slope = jnp.exp(values * values * -0.5) * 0.3989422804014327
    return values * area, area + values * slope


def softmax_columns(scores):
    peak = jnp.max(scores, axis=0, keepdims=True)
    raised = jnp.exp(scores - peak)
    return (raised * (1.0 / jnp.sum(raised, axis=0, keepdims=True))).astype(BF16)


def staggered(items, produce, consume):
    held = None
    for item in items:
        made = produce(item)
        if held is not None:
            consume(*held)
        held = (item, made)
    consume(*held)


class Loads:
    def __init__(self, sources, targets, sems, ahead):
        self.copies = [
            pltpu.make_async_copy(source, target, sems.at[item])
            for item, (source, target) in enumerate(zip(sources, targets))
        ]
        self.ahead, self.started = ahead, 0
        self.reach(ahead)

    def reach(self, count):
        for copy in self.copies[self.started : count]:
            copy.start()
        self.started = max(self.started, min(count, len(self.copies)))

    def wait(self, *items):
        for item in items:
            self.reach(item + 1 + self.ahead)
            self.copies[item].wait()


class Stores:
    def __init__(self, sems):
        self.sems, self.copies = sems, []

    def send(self, source, target):
        copy = pltpu.make_async_copy(source, target, self.sems.at[len(self.copies)])
        copy.start()
        self.copies.append(copy)

    def close(self):
        for copy in self.copies:
            copy.wait()


def row(ref, index):
    return ref[pl.ds(index, 1), :].astype(F32)


def forward_kernel(*refs):
    (aux, norm, bias, dec_norm, dec_bias, *refs) = refs
    width, dec_hidden = norm.shape[1], refs[10].shape[1]
    up_bias, dec_up_bias, added = aux.at[0:1], aux.at[1:2, :dec_hidden], aux.at[2:3, :width]
    load_hbm, refs = refs[:12], refs[12:]
    store_hbm, refs = refs[:20], refs[20:]
    load_vmem, refs = refs[:12], refs[12:]
    (
        tokens, qkv_w, out_w, up_w, down_w, embed_w, places, pos, dec_qkv_w, dec_out_w, dec_up_w,
        dec_down_w,
    ) = load_vmem
    enc_kept, dec_kept = refs[:10], refs[10:19]
    (decoded, embedded, values_t, load_sems, store_sems, block_sems, decoded_sems) = refs[19:]
    part = lax.axis_index("section")
    sources = list(load_hbm)
    sources[0] = sources[0].at[part, 0]
    sources[6] = sources[6].at[part]
    loads = Loads(sources, load_vmem, load_sems, 3)
    stores = Stores(store_sems)
    encode_rows(
        loads, stores, enc_kept, store_hbm[:10], tokens, added, norm, bias, up_bias, qkv_w,
        out_w, up_w, down_w,
    )
    loads.wait(5)
    embedded[...] = dot(enc_kept[-1][...], embed_w[...]) + row(dec_bias, 0)
    loads.wait(6, 7, 8)
    decode_rows(
        loads, stores, dec_kept, store_hbm[10:], embedded, places, pos, dec_norm, dec_bias,
        dec_up_bias, dec_qkv_w, dec_out_w, dec_up_w, dec_down_w, decoded, values_t, block_sems,
        decoded_sems,
    )
    stores.close()


def encode_rows(
    loads, stores, kept, kept_hbm, tokens, added, norm, bias, up_bias, qkv_w, out_w, up_w, down_w
):
    start_out, normed_out, packed, probs_out, attended_out, middle_out, second_out, active, slopes, encoded = kept

    def keep(item):
        stores.send(kept[item], kept_hbm[item])

    inner = out_w.shape[0]
    loads.wait(0)
    start = tokens[...].astype(F32) + added[...]
    start_out[...] = start
    keep(0)
    normed = (normalize(start)[0] * row(norm, 0) + row(norm, 1)).astype(BF16)
    normed_out[...] = normed
    keep(1)
    loads.wait(1)
    packed[...] = dot(normed, qkv_w[...]).astype(BF16)
    keep(2)
    columns = []
    heads = LANES // HEAD_DIM
    for group in range(inner // LANES):
        base = group * LANES
        queries = packed[:, base : base + LANES] * jnp.asarray(HEAD_DIM**-0.5, BF16)
        keys = packed[:, inner + base : inner + base + LANES]
        values = packed[:, 2 * inner + base : 2 * inner + base + LANES].T

        def weigh(head, scores, group=group, values=values):
            probs = softmax_columns(scores)
            probs_out[group * heads + head] = probs
            columns.append(dot(values[head * HEAD_DIM : (head + 1) * HEAD_DIM], probs).astype(BF16))

        staggered(
            range(heads),
            lambda head, keys=keys, queries=queries: dot_nt(keys, only_head(queries, head)),
            weigh,
        )
    keep(3)
    attended = jnp.concatenate(columns, axis=0).T
    attended_out[...] = attended
    keep(4)
    loads.wait(2)
    middle = start + (dot(attended, out_w[...]) + row(bias, 0))
    middle_out[...] = middle
    keep(5)
    second = (normalize(middle)[0] * row(norm, 2) + row(norm, 3)).astype(BF16)
    second_out[...] = second
    keep(6)
    loads.wait(3)
    panel = 768

    def bend(low, lifted):
        cols = slice(low, low + panel)
        raised, slope = gelu_pair(lifted + up_bias[:, cols].astype(F32))
        active[:, cols] = raised.astype(BF16)
        slopes[:, cols] = slope.astype(BF16)

    staggered(
        range(0, up_w.shape[1], panel), lambda low: dot(second, up_w[:, low : low + panel]), bend
    )
    keep(7)
    keep(8)
    loads.wait(4)
    encoded[...] = (middle + row(bias, 1) + dot(active[...], down_w[...])).astype(BF16)
    keep(9)


def decode_rows(
    loads, stores, kept, kept_hbm, embedded, places, pos, norm, bias, up_bias, qkv_w, out_w, up_w,
    down_w, decoded, values_t, block_sems, decoded_sems,
):
    placed, normed, packed, probs, attended, middle, second, active, slopes = kept
    length = pos.shape[0]
    inner = out_w.shape[0]
    visible = embedded.shape[0]
    heads = inner // HEAD_DIM
    blocks = length // BLOCK
    high = embedded[...].astype(BF16)
    rest = (embedded[...] - high.astype(F32)).astype(BF16)
    spots = places[:, pl.ds(0, visible)]

    def place(block):
        hit = lax.broadcasted_iota(jnp.int32, (BLOCK, visible), 0) + block * BLOCK == spots
        pick = jnp.where(hit, 1.0, 0.0).astype(BF16)
        seen = jnp.sum(jnp.where(hit, 1.0, 0.0), axis=1, keepdims=True)
        return dot(pick, high) + dot(pick, rest) + (1.0 - seen) * row(bias, 3)

    def begin(block, here):
        rows = slice(block * BLOCK, (block + 1) * BLOCK)
        here = here + pos[rows, :].astype(F32)
        placed[rows, :] = here
        norm_here = (normalize(here)[0] * row(norm, 0) + row(norm, 1)).astype(BF16)
        normed[rows, :] = norm_here
        packed[rows, :] = dot(norm_here, qkv_w[...]).astype(BF16)

    staggered(range(blocks), place, begin)
    for item in range(3):
        stores.send(kept[item], kept_hbm[1 + item])
    values_t[...] = packed[:, 2 * inner :].T
    loads.wait(9, 10, 11)
    bound = [(source, target) for source, target in zip(kept[3:], kept_hbm[4:])]

    def second_pass(block, carry):
        base = pl.multiple_of(block * BLOCK, BLOCK)
        rows = pl.ds(base, BLOCK)
        slot = lax.rem(block, 2)

        def out_copy(spot):
            return pltpu.make_async_copy(
                decoded.at[lax.rem(spot, 2)],
                kept_hbm[0].at[pl.ds(pl.multiple_of(spot * BLOCK, BLOCK), BLOCK)],
                decoded_sems.at[lax.rem(spot, 2)],
            )

        queries = packed[rows, :inner] * jnp.asarray(HEAD_DIM**-0.5, BF16)
        keys = packed[:, inner : 2 * inner]
        columns = []

        def weigh(head, scores):
            probs_here = softmax_columns(scores)
            probs[block, :, pl.ds(head * BLOCK, BLOCK)] = probs_here
            columns.append(
                dot(values_t[head * HEAD_DIM : (head + 1) * HEAD_DIM, :], probs_here).astype(BF16)
            )

        staggered(range(heads), lambda head: dot_nt(keys, only_head(queries, head)), weigh)
        attended_here = jnp.concatenate(columns, axis=0).T
        attended[rows, :] = attended_here
        middle_here = placed[rows, :] + (dot(attended_here, out_w[...]) + row(bias, 1))
        middle[rows, :] = middle_here
        second_here = (normalize(middle_here)[0] * row(norm, 2) + row(norm, 3)).astype(BF16)
        second[rows, :] = second_here
        panel = 512

        def bend(low, lifted):
            cols = slice(low, low + panel)
            raised, slope = gelu_pair(lifted + up_bias[:, cols].astype(F32))
            active[rows, cols] = raised.astype(BF16)
            slopes[rows, cols] = slope.astype(BF16)

        staggered(
            range(0, up_w.shape[1], panel),
            lambda low: dot(second_here, up_w[:, low : low + panel]),
            bend,
        )

        @pl.when(block >= 2)
        def _():
            out_copy(block - 2).wait()

        decoded[slot] = middle_here + (dot(active[rows, :], down_w[...]) + row(bias, 2))
        out_copy(block).start()
        for item, (source, target) in enumerate(bound):
            spot = rows if item else block
            pltpu.make_async_copy(source.at[spot], target.at[spot], block_sems.at[item]).start()

        @pl.when(block == blocks - 1)
        def _():
            out_copy(block - 1).wait()
            out_copy(block).wait()

        return carry

    lax.fori_loop(0, blocks, second_pass, 0)
    for item, (source, target) in enumerate(bound):
        pltpu.make_async_copy(source, target, block_sems.at[item]).wait()


WHOLE = pl.BlockSpec(memory_space=pltpu.VMEM)
APART = pl.BlockSpec(memory_space=pl.ANY)
LIMIT = pltpu.CompilerParams(vmem_limit_bytes=63 * 2**20)


def like(array):
    return pltpu.VMEM(array.shape, array.dtype)


def run_forward(tokens, order, aux, enc_w, dec_w):
    norm, qkv_w, out_w, bias, up_w, up_bias, down_w, table = enc_w
    embed_w, dec_norm, dec_qkv_w, dec_out_w, dec_bias, dec_up_w, dec_up_bias, dec_down_w, pos = dec_w
    rows, width = tokens.shape[2:]
    inner, hidden = out_w.shape[0], up_w.shape[1]
    shaped = jax.ShapeDtypeStruct
    enc_kept = [
        shaped((rows, width), F32),
        shaped((rows, width), BF16),
        shaped((rows, 3 * inner), BF16),
        shaped((inner // HEAD_DIM, rows, rows), BF16),
        shaped((rows, inner), BF16),
        shaped((rows, width), F32),
        shaped((rows, width), BF16),
        shaped((rows, hidden), BF16),
        shaped((rows, hidden), BF16),
        shaped((rows, width), BF16),
    ]
    length, dec_width = pos.shape
    dec_inner, dec_hidden = dec_out_w.shape[0], dec_up_w.shape[1]
    blocks = length // BLOCK
    dec_kept = [
        shaped((length, dec_width), F32),
        shaped((length, dec_width), BF16),
        shaped((length, 3 * dec_inner), BF16),
        shaped((blocks, length, dec_inner // HEAD_DIM * BLOCK), BF16),
        shaped((length, dec_inner), BF16),
        shaped((length, dec_width), F32),
        shaped((length, dec_width), BF16),
        shaped((length, dec_hidden), BF16),
        shaped((length, dec_hidden), BF16),
    ]
    weights = [
        qkv_w, out_w, up_w, down_w, embed_w, pos, dec_qkv_w, dec_out_w, dec_up_w, dec_down_w
    ]
    held = [like(item) for item in weights]
    results = pl.pallas_call(
        forward_kernel,
        out_shape=enc_kept + [shaped((length, dec_width), F32)] + dec_kept,
        in_specs=[WHOLE] * 5 + [APART] * 12,
        out_specs=[APART] * 20,
        scratch_shapes=[pltpu.VMEM((rows, width), BF16)]
        + held[:5]
        + [pltpu.VMEM((1, length), jnp.int32)]
        + held[5:]
        + [like(item) for item in enc_kept + dec_kept]
        + [
            pltpu.VMEM((2, BLOCK, dec_width), F32),
            pltpu.VMEM((rows, dec_width), F32),
            pltpu.VMEM((dec_inner, length), BF16),
            pltpu.SemaphoreType.DMA((12,)),
            pltpu.SemaphoreType.DMA((13,)),
            pltpu.SemaphoreType.DMA((6,)),
            pltpu.SemaphoreType.DMA((2,)),
        ],
        compiler_params=LIMIT,
        name="forward",
    )(
        aux,
        norm,
        bias,
        dec_norm,
        dec_bias,
        tokens,
        *weights[:5],
        order,
        *weights[5:],
    )
    return results[:9], results[9], results[10], results[11:]


def column_sum(values):
    return jnp.sum(values, axis=0, keepdims=True)


def norm_back(grad, values, scale):
    normal, inverse = normalize(values)
    inner = grad * scale
    mean_inner = jnp.mean(inner, axis=-1, keepdims=True)
    mean_both = jnp.mean(inner * normal, axis=-1, keepdims=True)
    return (
        inverse * (inner - mean_inner - normal * mean_both),
        column_sum(grad * normal),
        column_sum(grad),
    )


def attention_back(queries, keys, values, keys_t, probs, grad_rows, attended):
    block = queries.shape[0]
    heads = LANES // HEAD_DIM
    product = (grad_rows.astype(F32) * attended.astype(F32)).T
    scores_back, query_grads = [], []

    def through(head, probs_back):
        lanes = slice(head * HEAD_DIM, (head + 1) * HEAD_DIM)
        row_dots = column_sum(product[lanes])
        probs_here = probs[:, head * block : (head + 1) * block].astype(F32)
        scores_here = (probs_here * (probs_back - row_dots)).astype(BF16)
        scores_back.append(scores_here)
        query_grads.append(dot(keys_t[lanes], scores_here))

    staggered(range(heads), lambda head: dot_nt(values, only_head(grad_rows, head)), through)
    stacked_grad = jnp.concatenate([only_head(grad_rows, head) for head in range(heads)], axis=0)
    stacked_queries = jnp.concatenate([only_head(queries, head) for head in range(heads)], axis=0)
    grad_values = dot(probs, stacked_grad)
    grad_keys = dot(jnp.concatenate(scores_back, axis=1), stacked_queries)
    grad_queries = jnp.concatenate(query_grads, axis=0).T
    return grad_queries, grad_keys, grad_values


class Plan:
    def __init__(self, bits, blocks):
        self.bits, self.steps = bits, bits + 1
        self.waves, self.cuts = [], []
        orders, loads = orders_of(bits), [0.0, 0.0, 0.0]
        for rows, width in blocks:
            waves = []
            for wave in wave_plan(rows, width, orders, loads):
                waves.append([])
                for row_cut, col_cut, which in wave:
                    waves[-1].append((len(self.cuts), row_cut, col_cut, orders[which][0]))
                    self.cuts.append((row_cut[1], col_cut[1]))
            self.waves.append(waves)

    def scratch(self):
        lands = [
            pltpu.VMEM((2,) * (self.bits - step) + cut, BF16)
            for cut in self.cuts
            for step in range(self.steps)
        ]
        sems = pltpu.SemaphoreType.DMA((len(self.cuts), self.steps))
        return lands + [sems, sems]

    def scratch_count(self):
        return len(self.cuts) * self.steps + 2

    def bind(self, refs):
        self.refs = refs

    def chunks(self, slot, source, result):
        send_sems, recv_sems = self.refs[-2:]
        return [
            [
                Chunk(
                    source,
                    rows,
                    cols,
                    order,
                    self.refs[item * self.steps : (item + 1) * self.steps],
                    send_sems.at[item],
                    recv_sems.at[item],
                    result,
                )
                for item, rows, cols, order in wave
            ]
            for wave in self.waves[slot]
        ]


def fold(values, target):
    return values.astype(BF16).reshape(target.shape[:-1] + (values.shape[-1],))


def decode_back_kernel(plan, bits, *refs):
    (cotangent_hbm, places_hbm, norm, *refs) = refs
    load_hbm, refs = refs[:15], refs[15:]
    (returned, qkv_out, pos_out, embed_out, norm_sum, bias_sum, up_sum, *refs) = refs
    (down_done, up_done, out_done, *refs) = refs
    (cotangent, places, *refs) = refs
    load_vmem, refs = refs[:15], refs[15:]
    (
        active, down_w, slope, second, up_w, middle, attended, out_w, probs, packed,
        normed, placed, qkv_w, encoded, embed_w,
    ) = load_vmem
    (down_grad, up_grad, out_grad, grad_middle, attn_grad, grad_rows, grad_keys, grad_values,
     grad_packed, picked, load_sems, *refs) = refs
    plan.bind(refs)
    greet(bits)
    part = lax.axis_index("section")
    loads = Loads(
        [cotangent_hbm.at[part, 0], places_hbm.at[part], *load_hbm],
        [cotangent, places, *load_vmem],
        load_sems,
        6,
    )
    names = [
        "cotangent", "places", "active", "down_w", "slope", "second", "up_w", "middle", "attended",
        "out_w", "probs", "packed", "normed", "placed", "qkv_w", "encoded", "embed_w",
    ]

    def need(*wanted):
        loads.wait(*[names.index(item) for item in wanted])

    length, width = placed.shape
    inner, hidden = out_w.shape[0], up_w.shape[1]
    visible = encoded.shape[0]
    blocks = length // BLOCK
    flow = Flow(bits + 1, 2)

    def send(slot, source, result):
        for wave in plan.chunks(slot, source, result):
            flow.add(wave)

    need("cotangent", "active")
    panel = hidden // 4
    for item in range(4):
        cols = slice(item * panel, (item + 1) * panel)
        piece = dot(active[:, cols].T, cotangent[...]).astype(BF16)
        target = down_grad.at[item // 2, item % 2]
        target[...] = piece.reshape(target.shape)
    greeted(bits)
    send(0, down_grad, down_done)
    bias_sum[0:1, :] = jnp.zeros((1, width), F32)
    bias_sum[2:3, :] = column_sum(cotangent[...].astype(F32))
    need("down_w", "slope", "up_w", "middle", "out_w", "second")

    def lift_back(block):
        rows = slice(block * BLOCK, (block + 1) * BLOCK)
        lifted_back = dot_nt(cotangent[rows, :], down_w[...]) * slope[rows, :].astype(F32)
        lifted_back = lifted_back.astype(BF16)
        slope[rows, :] = lifted_back
        up_part = column_sum(lifted_back.astype(F32))
        up_sum[...] = up_part + up_sum[...] if block else up_part
        return dot_nt(lifted_back, up_w[...])

    def middle_back(block, grad_second):
        rows = slice(block * BLOCK, (block + 1) * BLOCK)
        inward, scale_part, shift_part = norm_back(grad_second, middle[rows, :], row(norm, 2))
        total = cotangent[rows, :].astype(F32) + inward
        grad_middle[rows, :] = total
        rounded = total.astype(BF16)
        attn_grad[rows, :] = rounded
        bias_part = column_sum(rounded.astype(F32))
        grad_rows[rows, :] = dot_nt(rounded, out_w[...]).astype(BF16)
        if block:
            scale_part = scale_part + norm_sum[2:3, :]
            shift_part = shift_part + norm_sum[3:4, :]
            bias_part = bias_part + bias_sum[1:2, :]
        norm_sum[2:3, :] = scale_part
        norm_sum[3:4, :] = shift_part
        bias_sum[1:2, :] = bias_part
        if block % 2:
            flow.tick()

    staggered(range(blocks), lift_back, middle_back)
    second_t = second[...].T
    for item in range(4):
        cols = slice(item * panel, (item + 1) * panel)
        up_grad[:, :, :, :, :, cols] = fold(dot(second_t, slope[:, cols]), up_grad)
    send(1, up_grad, up_done)
    need("attended")
    out_grad[...] = fold(dot(attended[...].T, attn_grad[...]), out_grad)
    send(2, out_grad, out_done)
    need("probs", "packed")
    keys = packed[:, inner : 2 * inner]
    values = packed[:, 2 * inner :]
    keys_t = keys.T
    scale = HEAD_DIM**-0.5
    for block in range(blocks):
        rows = slice(block * BLOCK, (block + 1) * BLOCK)
        query_part, key_part, value_part = attention_back(
            packed[rows, :inner], keys, values, keys_t, probs[block], grad_rows[rows, :],
            attended[rows, :],
        )
        grad_packed[rows, :inner] = (query_part * scale).astype(BF16)
        if block:
            key_part = key_part + grad_keys[...]
            value_part = value_part + grad_values[...]
        if block < blocks - 1:
            grad_keys[...] = key_part
            grad_values[...] = value_part
        else:
            grad_packed[:, inner : 2 * inner] = (key_part * scale).astype(BF16)
            grad_packed[:, 2 * inner :] = value_part.astype(BF16)
        flow.tick()
    need("normed", "placed", "qkv_w", "places")
    qkv_out[...] = fold(dot(normed[...].T, grad_packed[...]), qkv_out)
    flow.tick()
    spots = places[:, pl.ds(0, visible)]

    def start_back(block, grad_normed):
        rows = slice(block * BLOCK, (block + 1) * BLOCK)
        inward, scale_part, shift_part = norm_back(grad_normed, placed[rows, :], row(norm, 0))
        total = grad_middle[rows, :] + inward
        hit = lax.broadcasted_iota(jnp.int32, (BLOCK, visible), 0) + block * BLOCK == spots
        pick = jnp.where(hit, 1.0, 0.0).astype(BF16)
        seen = jnp.sum(jnp.where(hit, 1.0, 0.0), axis=1, keepdims=True)
        fill_part = column_sum(total * (1.0 - seen))
        rounded = total.astype(BF16)
        pick_part = dot(pick.T, rounded)
        if block:
            scale_part = scale_part + norm_sum[0:1, :]
            shift_part = shift_part + norm_sum[1:2, :]
            fill_part = fill_part + bias_sum[3:4, :]
            pick_part = pick_part + picked[...]
        norm_sum[0:1, :] = scale_part
        norm_sum[1:2, :] = shift_part
        bias_sum[3:4, :] = fill_part
        picked[...] = pick_part
        pos_out[:, :, :, :, :, rows] = fold(rounded.T, pos_out)
        flow.tick()

    staggered(
        range(blocks),
        lambda block: dot_nt(grad_packed[block * BLOCK : (block + 1) * BLOCK, :], qkv_w[...]),
        start_back,
    )
    need("encoded", "embed_w")
    grad_embedded = picked[...].astype(BF16)
    bias_sum[0:1, :] = column_sum(picked[...])
    embed_out[...] = fold(dot(encoded[...].T, grad_embedded), embed_out)
    returned[...] = dot_nt(grad_embedded, embed_w[...]).astype(BF16)
    flow.drain()


def encode_back_kernel(plan, bits, *refs):
    (returned, aux, norm, dec_norm_sum, dec_bias_sum, dec_up_sum, *refs) = refs
    early, refs = refs[:3], refs[3:]
    load_hbm, refs = refs[:13], refs[13:]
    (input_grad, small_done, *refs) = refs
    done, refs = refs[:7], refs[7:]
    load_vmem, refs = refs[:13], refs[13:]
    (
        active, down_w, slope, second, up_w, middle, attended, out_w, probs, packed,
        normed, start, qkv_w,
    ) = load_vmem
    (down_grad, up_grad, out_grad, qkv_grad, grad_packed, small, small_lands, small_send,
     small_recv, load_sems, *refs) = refs
    plan.bind(refs)
    greet(bits)
    loads = Loads(load_hbm, load_vmem, load_sems, 6)
    names = [
        "active", "down_w", "slope", "second", "up_w", "middle", "attended", "out_w", "probs",
        "packed", "normed", "start", "qkv_w",
    ]

    def need(*wanted):
        loads.wait(*[names.index(item) for item in wanted])

    inner, hidden = out_w.shape[0], up_w.shape[1]
    width = start.shape[1]
    greeted(bits)
    flow = Flow(bits + 1, 2)

    def send(slot, source, result, part=None):
        waves = plan.chunks(slot, source, result)
        for wave in waves if part is None else waves[part : part + 1]:
            flow.add(wave)

    for slot, source in enumerate(early):
        send(slot, source, done[slot])
    branch = returned[...]
    small[...] = jnp.zeros_like(small)
    small[5:6, :] = column_sum(branch.astype(F32))
    need("active")
    panel = hidden // 4
    for item in range(4):
        cols = slice(item * panel, (item + 1) * panel)
        target = down_grad.at[item // 2, item % 2]
        target[...] = dot(active[:, cols].T, branch).astype(BF16).reshape(target.shape)
    flow.tick()
    send(3, down_grad, done[3], 0)
    need("second", "slope", "down_w")
    second_t = second[...].T
    for item in range(4):
        cols = slice(item * panel, (item + 1) * panel)
        lifted_back = (dot_nt(branch, down_w[cols, :]) * slope[:, cols].astype(F32)).astype(BF16)
        slope[:, cols] = lifted_back
        small[10 + item : 11 + item, :] = column_sum(lifted_back.astype(F32))
        up_grad[:, :, :, :, :, cols] = fold(dot(second_t, lifted_back), up_grad)
    flow.tick()
    send(3, down_grad, done[3], 1)
    need("up_w", "middle", "out_w", "attended")
    grad_second = dot_nt(slope[...], up_w[...])
    inward, small[2:3, :], small[3:4, :] = norm_back(grad_second, middle[...], row(norm, 2))
    grad_middle = branch.astype(F32) + inward
    attn_grad = grad_middle.astype(BF16)
    small[4:5, :] = column_sum(attn_grad.astype(F32))
    flow.tick()
    send(4, up_grad, done[4], 0)
    out_grad[...] = fold(dot(attended[...].T, attn_grad), out_grad)
    grad_rows = dot_nt(attn_grad, out_w[...]).astype(BF16)
    flow.tick()
    send(4, up_grad, done[4], 1)
    need("probs", "packed")
    scale = HEAD_DIM**-0.5
    heads = LANES // HEAD_DIM
    for group in range(inner // LANES):
        base = group * LANES
        lanes = slice(base, base + LANES)
        keys = packed[:, inner + base : inner + base + LANES]
        query_part, key_part, value_part = attention_back(
            packed[:, lanes],
            keys,
            packed[:, 2 * inner + base : 2 * inner + base + LANES],
            keys.T,
            jnp.concatenate([probs[group * heads + head] for head in range(heads)], axis=1),
            grad_rows[:, lanes],
            attended[:, lanes],
        )
        grad_packed[:, lanes] = (query_part * scale).astype(BF16)
        grad_packed[:, inner + base : inner + base + LANES] = (key_part * scale).astype(BF16)
        grad_packed[:, 2 * inner + base : 2 * inner + base + LANES] = value_part.astype(BF16)
    flow.tick()
    need("normed", "start", "qkv_w")
    send(5, out_grad, done[5])
    normed_t = normed[...].T
    for item in range(3):
        cols = slice(item * inner, (item + 1) * inner)
        qkv_grad[:, :, :, :, :, cols] = fold(dot(normed_t, grad_packed[:, cols]), qkv_grad)
    flow.tick()
    send(6, qkv_grad, done[6])
    grad_normed = dot_nt(grad_packed[...], qkv_w[...])
    inward, small[0:1, :], small[1:2, :] = norm_back(grad_normed, start[...], row(norm, 0))
    grad_start = grad_middle + inward
    input_grad[...] = grad_start
    small[6:10, :] = aux[4:8, : start.shape[1]] * column_sum(grad_start)
    dec_width = dec_norm_sum.shape[1]
    small[14:18, :dec_width] = dec_norm_sum[...]
    small[18:22, :dec_width] = dec_bias_sum[...]
    for item in range(4):
        small[22 + item : 23 + item, :dec_width] = dec_up_sum[
            :, item * dec_width : (item + 1) * dec_width
        ]
    flow.add([Whole(small, bits, small_lands, small_send, small_recv, small_done)])
    flow.drain()


def finish_kernel(counts, *refs):
    small_count, big_count = counts
    small, big, refs = refs[0], refs[1 : 1 + big_count], refs[1 + big_count :]
    tiny, big_out, sems = refs[:small_count], refs[small_count:-1], refs[-1]
    copies = [
        pltpu.make_async_copy(source, target, sems.at[item])
        for item, (source, target) in enumerate(zip(big, big_out))
    ]
    for copy in copies:
        copy.start()
    section, data = lax.axis_index("section"), lax.axis_index("dp")
    datas = lax.axis_size("dp")
    first = 0
    for out in tiny:
        cols = out.shape[-1]
        if out.shape[0] > 1 or first == 4:
            lines = out.shape[0]
            width = cols * datas
            here = jnp.where(
                section == 0,
                small[first : first + lines, :width],
                small[first + lines : first + 2 * lines, :width],
            )
            spot = data * cols
            first += 2 * lines
        else:
            lines = 4
            width = cols * datas * 2 // lines
            per_line = width // cols
            index = section * datas + data
            here = jnp.zeros((1, width), F32)
            for line in range(lines):
                mine = index // per_line == line
                here = here + jnp.where(mine, small[first + line : first + line + 1, :width], 0.0)
            spot = lax.rem(index, per_line) * cols
            first += lines
        here = pltpu.roll(here, lax.rem(width - spot, width), 1)
        out[...] = here[:, :cols]
    for copy in copies:
        copy.wait()


def run_finish(small, big, shapes):
    shaped = jax.ShapeDtypeStruct
    return pl.pallas_call(
        partial(finish_kernel, (len(shapes), len(big))),
        out_shape=[shaped(item, F32) for item in shapes]
        + [shaped(item.shape, F32) for item in big],
        in_specs=[WHOLE] + [APART] * len(big),
        out_specs=[WHOLE] * (len(shapes) + len(big)),
        scratch_shapes=[pltpu.SemaphoreType.DMA((len(big),))],
        name="finish",
    )(small, *big)


def communicating(number):
    return pltpu.CompilerParams(
        collective_id=number, has_side_effects=True, vmem_limit_bytes=63 * 2**20
    )


def blocked(rows, cols, bits):
    return (2,) * bits + (rows // 2**bits, cols)


def run_decode_back(cotangent, order, stored, encoded, dec_w, bits):
    embed_w, norm, qkv_w, out_w, bias, up_w, up_bias, down_w, pos = dec_w
    placed, normed, packed, probs, attended, middle, second, active, slope = stored
    length, width = pos.shape
    inner, hidden = out_w.shape[0], up_w.shape[1]
    shaped = jax.ShapeDtypeStruct
    loaded = [
        active, down_w, slope, second, up_w, middle, attended, out_w, probs, packed, normed,
        placed, qkv_w, encoded, embed_w,
    ]
    sent = [blocked(*item.shape, bits) for item in (down_w, up_w, out_w)]
    plan = Plan(bits, [(item[-2], item[-1] // 2) for item in sent])
    later = [blocked(*qkv_w.shape, bits), blocked(width, length, bits), blocked(*embed_w.shape, bits)]
    return pl.pallas_call(
        partial(decode_back_kernel, plan, bits),
        out_shape=[shaped(encoded.shape, BF16)]
        + [shaped(item, BF16) for item in later]
        + [shaped((4, width), F32), shaped((4, width), F32), shaped((1, hidden), F32)]
        + [shaped((item[-2], item[-1] // 2), F32) for item in sent],
        in_specs=[APART, APART, WHOLE] + [APART] * len(loaded),
        out_specs=[WHOLE] * 10,
        scratch_shapes=[
            pltpu.VMEM((length, width), BF16),
            pltpu.VMEM((1, length), jnp.int32),
        ]
        + [like(item) for item in loaded]
        + [pltpu.VMEM(item, BF16) for item in sent]
        + [
            pltpu.VMEM((length, width), F32),
            pltpu.VMEM((length, width), BF16),
            pltpu.VMEM((length, inner), BF16),
            pltpu.VMEM((length, inner), F32),
            pltpu.VMEM((length, inner), F32),
            pltpu.VMEM((length, 3 * inner), BF16),
            pltpu.VMEM((encoded.shape[0], width), F32),
            pltpu.SemaphoreType.DMA((len(loaded) + 2,)),
        ]
        + plan.scratch(),
        compiler_params=communicating(1),
        name="decode_back",
    )(cotangent, order, norm, *loaded)


def run_encode_back(returned, aux, stored, enc_w, early, dec_sums, bits):
    norm, qkv_w, out_w, bias, up_w, up_bias, down_w, table = enc_w
    start, normed, packed, probs, attended, middle, second, active, slope = stored
    shaped = jax.ShapeDtypeStruct
    loaded = [
        active, down_w, slope, second, up_w, middle, attended, out_w, probs, packed, normed,
        start, qkv_w,
    ]
    own = [blocked(*item.shape, bits) for item in (down_w, up_w, out_w, qkv_w)]
    sent = [item.shape for item in early] + own
    plan = Plan(bits, [(item[-2], item[-1] // 2) for item in sent])
    width = start.shape[1]
    small = (SMALL_ROWS, width)
    return pl.pallas_call(
        partial(encode_back_kernel, plan, bits),
        out_shape=[shaped(start.shape, F32), shaped(small, F32)]
        + [shaped((item[-2], item[-1] // 2), F32) for item in sent],
        in_specs=[WHOLE] * 9 + [APART] * len(loaded),
        out_specs=[WHOLE] * 9,
        scratch_shapes=[like(item) for item in loaded]
        + [pltpu.VMEM(item, BF16) for item in own]
        + [
            pltpu.VMEM(packed.shape, BF16),
            pltpu.VMEM(small, F32),
            pltpu.VMEM((bits + 1,) + small, F32),
            pltpu.SemaphoreType.DMA((bits + 1,)),
            pltpu.SemaphoreType.DMA((bits + 1,)),
            pltpu.SemaphoreType.DMA((len(loaded),)),
        ]
        + plan.scratch(),
        compiler_params=communicating(2),
        name="encode_back",
    )(returned, aux, norm, *dec_sums, *early, *loaded)


def local_rows(whole, shape):
    section, data = lax.axis_index("section"), lax.axis_index("dp")
    sections, datas = lax.axis_size("section"), lax.axis_size("dp")
    if len(shape) == 1:
        count = shape[0] // (sections * datas)
        return lax.dynamic_slice_in_dim(
            whole.reshape(-1)[: shape[0]], (section * datas + data) * count, count, 0
        )
    rows, cols = shape[0] // sections, shape[1] // datas
    return lax.dynamic_slice(whole, (section * rows, data * cols), (rows, cols))


def plain_shards(tokens, order, sensor, cotangent, enc_w, dec_w):
    section_count = lax.axis_size("section")
    section_index = lax.axis_index("section")
    half_count = tokens.shape[0] // section_count

    def mine(array):
        part = lax.dynamic_slice_in_dim(array, section_index * half_count, half_count, 0)
        return part.reshape((half_count * array.shape[1],) + array.shape[2:])

    encoded, stored, picks = encode(mine(tokens), mine(sensor), enc_w)
    output, returned, dec_grads = decode(encoded, mine(order), mine(cotangent), dec_w)
    grad_input, enc_grads = encode_back(stored, picks, returned, enc_w)
    done = []
    for slot, grad in enumerate(enc_grads + dec_grads):
        if slot in (0, 3, 5, 7, 9, 12, 14):
            total = local_rows(lax.psum(grad, ("section", "dp")), grad.shape)
        else:
            side = 0 if slot == 16 else 1
            total = lax.psum_scatter(
                grad.astype(jnp.bfloat16), "section", scatter_dimension=side, tiled=True
            )
            total = lax.psum_scatter(total, "dp", scatter_dimension=1 - side, tiled=True)
        done.append(total.astype(jnp.float32))
    decoded = output.reshape((half_count,) + cotangent.shape[1:])
    input_grad = grad_input.reshape((half_count,) + tokens.shape[1:])
    return (decoded, input_grad) + tuple(done)


def shards(tokens, order, sensor, cotangent, *weights):
    enc_w, dec_w = weights[:8], weights[8:]
    sections, datas = lax.axis_size("section"), lax.axis_size("dp")
    split_rows = [enc_w[1], enc_w[2], enc_w[4], enc_w[6], dec_w[0], dec_w[2], dec_w[3], dec_w[5]]
    fits = (
        sections == 2
        and tokens.shape[:2] == (sections, 1)
        and datas & (datas - 1) == 0
        and datas >= 4
        and all(item.shape[0] % (16 * datas) == 0 for item in split_rows)
    )
    if not fits:
        return plain_shards(tokens, order, sensor, cotangent, enc_w, dec_w)
    bits = datas.bit_length() - 1
    kind = lax.dynamic_index_in_dim(sensor, lax.axis_index("section"), 0, keepdims=False)
    kinds = (jnp.arange(enc_w[7].shape[0]) == kind).astype(F32)[:, None]
    hidden = enc_w[4].shape[1]

    def wide(item):
        return jnp.pad(item, ((0, 0), (0, hidden - item.shape[1])))

    aux = jnp.concatenate(
        [
            enc_w[5].astype(F32)[None],
            wide(dec_w[6].astype(F32)[None]),
            wide(jnp.sum(kinds * enc_w[7].astype(F32), axis=0, keepdims=True)),
            jnp.zeros((1, hidden), F32),
            jnp.broadcast_to(kinds, (kinds.shape[0], hidden)),
        ]
    )
    enc_kept, encoded, decoded, dec_kept = run_forward(tokens, order, aux, enc_w, dec_w)
    back = run_decode_back(cotangent, order, dec_kept, encoded, dec_w, bits)
    returned, early, dec_sums, dec_done = back[0], back[1:4], back[4:7], back[7:]
    down_dec, up_dec, out_dec = dec_done
    input_grad, small, *rest = run_encode_back(
        returned, aux, enc_kept, enc_w, early, dec_sums, bits
    )
    qkv_dec, pos, embed, down, up, out, qkv = rest
    tiny_slots = (0, 3, 7, 5, 9, 12, 14)
    shapes = [
        (item.shape[0] // 2, item.shape[1] // datas)
        if item.ndim == 2
        else (1, item.shape[0] // (2 * datas))
        for item in (weights[slot] for slot in tiny_slots)
    ]
    large = {
        1: qkv, 2: out, 4: up, 6: down, 8: embed, 10: qkv_dec, 11: out_dec, 13: up_dec, 15: down_dec,
        16: pos,
    }
    results = run_finish(small, [input_grad, *large.values()], shapes)
    done = dict(zip([*tiny_slots, "input", *large], results))
    for slot in (5, 14):
        done[slot] = done[slot].reshape(-1)
    done[16] = done[16].T
    return (decoded[None, None], done["input"][None, None]) + tuple(
        done[slot] for slot in range(17)
    )


def solution(mesh):
    placed = (
        P(None, "dp", None, None),
        P(None, "dp", None),
        P(None, "dp"),
        P(None, "dp", None, None),
        P(),
        P(),
        P(),
        P(),
        P(),
        P(),
        P(),
        P(),
        P(),
        P(),
        P(),
        P(),
        P(),
        P(),
        P(),
        P(),
        P(),
    )
    return jax.shard_map(
        shards,
        mesh=mesh,
        in_specs=placed,
        out_specs=(
            P("section", "dp", None, None),
            P("section", "dp", None, None),
            P("section", "dp"),
            P("dp", "section"),
            P("dp", "section"),
            P("section", "dp"),
            P("dp", "section"),
            P(("section", "dp")),
            P("dp", "section"),
            P("section", "dp"),
            P("dp", "section"),
            P("section", "dp"),
            P("dp", "section"),
            P("dp", "section"),
            P("section", "dp"),
            P("dp", "section"),
            P(("section", "dp")),
            P("dp", "section"),
            P("section", "dp"),
        ),
        check_vma=False,
    )
```

profile of v0, /device:TPU:0, one launch (start us, length us, event | category | flops | bytes accessed | tf_op | source)
XLA Modules:
  0.0 183.9 jit_solution(6335473318574167989)
XLA Ops:
  0.7 0.0 copy-start
  0.7 0.6 copy-done
  1.3 0.6 constant_dynamic-slice_fusion
  1.9 0.6 compare_convert_fusion
  2.6 0.8 multiply_reduce_fusion
  3.3 0.7 broadcast_in_dim.30
  4.1 0.7 broadcast_in_dim.36
  4.8 0.1 broadcast_in_dim.33
  4.9 0.7 concatenate.3.refs_0_.refs_1_
  5.6 46.0 %forward.1 = (f32[256,768]{1,0:T(8,128)}, bf16[256,768]{1,0:T(8,128)(2,1)}, bf16[256,2304]{1,0:T(8,128)(2,1)}, bf16[12,256,256]{2,1,0:T(8,128)(2,1)}, bf16[256,7...) custom-call(f32[8,3072]{1,0:T(8,128)} %concatenate.3.refs_0_.refs_1_, ...), custom_call_target="tpu_custom_call" | custom-call | tf_op jit(solution)/shard_map/forward/pallas_call | solution.py:760
  51.6 47.1 %decode_back.1 = (bf16[256,768]{1,0:T(8,128)(2,1)}, bf16[2,2,2,2,32,768]{5,4,3,2,1,0:T(8,128)(2,1)}, bf16[2,2,2,2,32,1024]{5,4,3,2,1,0:T(8,128)(2,1)}, bf16[2,2,...) custom-call(bf16[2,1,1024,512]{3,2,1,0:T(8,128)(2,1)} %refs_0_.1, ...), custom_call_target="tpu_custom_call" | custom-call | tf_op jit(solution)/shard_map/decode_back/pallas_call | solution.py:1230
  98.7 0.0 copy-start.1
  98.7 81.1 %encode_back.1 = (f32[256,768]{1,0:T(8,128)}, f32[32,768]{1,0:T(8,128)}, f32[32,384]{1,0:T(8,128)}, f32[32,512]{1,0:T(8,128)}, f32[48,256]{1,0:T(8,128)}, /*inde...) custom-call(bf16[256,768]{1,0:T(8,128)(2,1)} %get-tuple-element.87.refs_0_, ...), custom_call_target="tpu_custom_call" | custom-call | tf_op jit(solution)/shard_map/encode_back/pallas_call | solution.py:1273
  179.8 3.9 %finish.1 = (f32[2,48]{1,0:T(2,128)}, f32[1,48]{1,0:T(1,128)}, f32[2,48]{1,0:T(2,128)}, f32[1,96]{1,0:T(1,128)}, f32[2,32]{1,0:T(2,128)}, /*index=5*/f32[2,32]{1...) custom-call(f32[32,768]{1,0:T(8,128)} %get-tuple-element.103.refs_0_, ...), custom_call_target="tpu_custom_call" | custom-call | tf_op jit(solution)/shard_map/finish/pallas_call | solution.py:1196
  183.7 0.0 copy-done.1
  (4 shorter events, 0.0 us)
Async XLA Ops:
  0.7 0.7 copy-start
  98.7 85.0 %copy-start.1 = (s32[2,1]{0,1:T(1,128)S(1)}, s32[2,1]{0,1:T(1,128)}, u32[]{:S(2)}) copy-start(s32[2,1]{0,1:T(1,128)} %param.23) | copy-start | bytes 28
where the time goes:
time: 186 us; the launch traced here: 184 us
  Pallas kernels  178 us (96%)
  local copies, waits for them, and re-layouts  2.76 us (1%)
  other arithmetic  2.13 us (1%)
    pallas_call x1, Pallas kernels, run_encode_back(): pl.pallas_call(partial(encode_back_kernel, plan, bits), out_shape=[shaped...  81.1 us
    pallas_call x1, Pallas kernels, run_decode_back(): pl.pallas_call(partial(decode_back_kernel, plan, bits), out_shape=[shaped...  47.1 us
    pallas_call x1, Pallas kernels, run_forward(): pl.pallas_call(forward_kernel, out_shape=enc_kept + [shaped((length, dec_...  46 us
    pallas_call x1, Pallas kernels, run_finish(): pl.pallas_call(partial(finish_kernel, (len(shapes), len(big))), out_shape...  3.89 us

commit v1 on v0

--- a/solution.py
+++ b/solution.py
@@ -261,11 +261,10 @@
 
 
 class Chunk:
-    def __init__(self, source, rows, cols, stages, lands, send_sems, recv_sems, result):
+    def __init__(self, source, rows, cols, stages, dims, lands, send_sems, recv_sems, result):
         self.source, self.rows, self.cols, self.stages = source, rows, cols, stages
         self.lands, self.send_sems, self.recv_sems = lands, send_sems, recv_sems
-        self.result = result
-        self.dims = list(range(len(stages) - 2, -1, -1))
+        self.result, self.dims = result, dims
 
     def halves(self, step):
         stage = self.stages[step]
@@ -282,8 +281,8 @@
                 ]
 
             return part(1 - bit), part(bit)
-        held = self.lands[step - 1]
-        left = [item for item in self.dims if item not in self.stages[1:step]]
+        held = self.lands[step - 1] if step else self.source
+        left = [item for item in self.dims if item not in self.stages[:step]]
         place = left.index(stage)
 
         def part(side):
@@ -295,8 +294,8 @@
         return pltpu.make_async_remote_copy(
             src_ref=self.halves(step)[0],
             dst_ref=self.lands[step],
-            send_sem=self.send_sems.at[step],
-            recv_sem=self.recv_sems.at[step],
+            send_sem=self.send_sems[step],
+            recv_sem=self.recv_sems[step],
             device_id=partner_of(self.stages[step]),
             device_id_type=MESH,
         )
@@ -307,9 +306,11 @@
     def finish(self, step):
         self.copy(step).wait_recv()
         kept, land = self.halves(step)[1], self.lands[step]
-        if len(land.shape) > 2:
+        if step + 1 < len(self.stages):
             land[...] = land[...] + kept[...]
             self.start(step + 1)
+        elif len(land.shape) > 2:
+            self.result[...] = land[...] + kept[...]
         else:
             self.result[pl.ds(*self.rows), pl.ds(*self.cols)] = land[...].astype(
                 jnp.float32
@@ -357,9 +358,8 @@
 
 
 class Flow:
-    def __init__(self, steps, lag):
-        self.steps, self.lag = steps, lag
-        self.waves, self.tick_now = [], 0
+    def __init__(self, lag):
+        self.lag, self.waves, self.tick_now = lag, [], 0
 
     def add(self, chunks):
         for chunk in chunks:
@@ -370,16 +370,16 @@
         self.tick_now += 1
         for wave in self.waves:
             chunks, step, due = wave
-            if step < self.steps and due <= self.tick_now:
+            if step < len(chunks[0].stages) and due <= self.tick_now:
                 for chunk in chunks:
                     chunk.finish(step)
                 wave[1], wave[2] = step + 1, self.tick_now + self.lag
 
     def drain(self):
-        while any(wave[1] < self.steps for wave in self.waves):
+        while any(step < len(chunks[0].stages) for chunks, step, _ in self.waves):
             self.tick()
-        for wave in self.waves:
-            for chunk in wave[0]:
+        for chunks, _, _ in self.waves:
+            for chunk in chunks:
                 chunk.close()
 
 
@@ -506,14 +506,16 @@
             copy.wait()
 
 
+def line(ref, cols):
+    return ref[cols].astype(F32).reshape(1, -1)
+
+
 def row(ref, index):
     return ref[pl.ds(index, 1), :].astype(F32)
 
 
 def forward_kernel(*refs):
-    (aux, norm, bias, dec_norm, dec_bias, *refs) = refs
-    width, dec_hidden = norm.shape[1], refs[10].shape[1]
-    up_bias, dec_up_bias, added = aux.at[0:1], aux.at[1:2, :dec_hidden], aux.at[2:3, :width]
+    (sensor, norm, bias, up_bias, table, dec_norm, dec_bias, dec_up_bias, *refs) = refs
     load_hbm, refs = refs[:12], refs[12:]
     store_hbm, refs = refs[:20], refs[20:]
     load_vmem, refs = refs[:12], refs[12:]
@@ -530,8 +532,8 @@
     loads = Loads(sources, load_vmem, load_sems, 3)
     stores = Stores(store_sems)
     encode_rows(
-        loads, stores, enc_kept, store_hbm[:10], tokens, added, norm, bias, up_bias, qkv_w,
-        out_w, up_w, down_w,
+        loads, stores, enc_kept, store_hbm[:10], tokens, sensor[part], norm, bias, up_bias,
+        table, qkv_w, out_w, up_w, down_w,
     )
     loads.wait(5)
     embedded[...] = dot(enc_kept[-1][...], embed_w[...]) + row(dec_bias, 0)
@@ -545,7 +547,8 @@
 
 
 def encode_rows(
-    loads, stores, kept, kept_hbm, tokens, added, norm, bias, up_bias, qkv_w, out_w, up_w, down_w
+    loads, stores, kept, kept_hbm, tokens, kind, norm, bias, up_bias, table, qkv_w, out_w, up_w,
+    down_w,
 ):
     start_out, normed_out, packed, probs_out, attended_out, middle_out, second_out, active, slopes, encoded = kept
 
@@ -553,8 +556,11 @@
         stores.send(kept[item], kept_hbm[item])
 
     inner = out_w.shape[0]
+    added = jnp.zeros((1, table.shape[1]), F32)
+    for item in range(table.shape[0]):
+        added = added + jnp.where(kind == item, row(table, item), 0.0)
     loads.wait(0)
-    start = tokens[...].astype(F32) + added[...]
+    start = tokens[...].astype(F32) + added
     start_out[...] = start
     keep(0)
     normed = (normalize(start)[0] * row(norm, 0) + row(norm, 1)).astype(BF16)
@@ -597,7 +603,7 @@
 
     def bend(low, lifted):
         cols = slice(low, low + panel)
-        raised, slope = gelu_pair(lifted + up_bias[:, cols].astype(F32))
+        raised, slope = gelu_pair(lifted + line(up_bias, cols))
         active[:, cols] = raised.astype(BF16)
         slopes[:, cols] = slope.astype(BF16)
 
@@ -680,7 +686,7 @@
 
         def bend(low, lifted):
             cols = slice(low, low + panel)
-            raised, slope = gelu_pair(lifted + up_bias[:, cols].astype(F32))
+            raised, slope = gelu_pair(lifted + line(up_bias, cols))
             active[rows, cols] = raised.astype(BF16)
             slopes[rows, cols] = slope.astype(BF16)
 
@@ -714,6 +720,7 @@
 
 WHOLE = pl.BlockSpec(memory_space=pltpu.VMEM)
 APART = pl.BlockSpec(memory_space=pl.ANY)
+SCALARS = pl.BlockSpec(memory_space=pltpu.SMEM)
 LIMIT = pltpu.CompilerParams(vmem_limit_bytes=63 * 2**20)
 
 
@@ -721,7 +728,7 @@
     return pltpu.VMEM(array.shape, array.dtype)
 
 
-def run_forward(tokens, order, aux, enc_w, dec_w):
+def run_forward(tokens, order, sensor, enc_w, dec_w):
     norm, qkv_w, out_w, bias, up_w, up_bias, down_w, table = enc_w
     embed_w, dec_norm, dec_qkv_w, dec_out_w, dec_bias, dec_up_w, dec_up_bias, dec_down_w, pos = dec_w
     rows, width = tokens.shape[2:]
@@ -760,7 +767,7 @@
     results = pl.pallas_call(
         forward_kernel,
         out_shape=enc_kept + [shaped((length, dec_width), F32)] + dec_kept,
-        in_specs=[WHOLE] * 5 + [APART] * 12,
+        in_specs=[SCALARS] + [WHOLE] * 7 + [APART] * 12,
         out_specs=[APART] * 20,
         scratch_shapes=[pltpu.VMEM((rows, width), BF16)]
         + held[:5]
@@ -779,11 +786,14 @@
         compiler_params=LIMIT,
         name="forward",
     )(
-        aux,
+        sensor,
         norm,
         bias,
+        up_bias,
+        table,
         dec_norm,
         dec_bias,
+        dec_up_bias,
         tokens,
         *weights[:5],
         order,
@@ -832,52 +842,69 @@
 
 
 class Plan:
-    def __init__(self, bits, blocks):
-        self.bits, self.steps = bits, bits + 1
-        self.waves, self.cuts = [], []
-        orders, loads = orders_of(bits), [0.0, 0.0, 0.0]
-        for rows, width in blocks:
-            waves = []
-            for wave in wave_plan(rows, width, orders, loads):
-                waves.append([])
-                for row_cut, col_cut, which in wave:
-                    waves[-1].append((len(self.cuts), row_cut, col_cut, orders[which][0]))
-                    self.cuts.append((row_cut[1], col_cut[1]))
-            self.waves.append(waves)
+    def __init__(self, bits, parts):
+        self.bits, self.parts = bits, parts
+        self.spans, count = [], 0
+        for waves, begin, end in parts:
+            for wave in waves:
+                for _ in wave:
+                    self.spans.append((count, count + end - begin))
+                    count += end - begin
+
+    def shape(self, cut, step):
+        rows, cols, _ = cut
+        return (2,) * (self.bits - step) + (rows[1], cols[1])
+
+    def cuts(self, slot):
+        return [cut for wave in self.parts[slot][0] for cut in wave]
+
+    def handed(self, slot):
+        return [self.shape(cut, self.parts[slot][2] - 1) for cut in self.cuts(slot)]
 
     def scratch(self):
         lands = [
-            pltpu.VMEM((2,) * (self.bits - step) + cut, BF16)
-            for cut in self.cuts
-            for step in range(self.steps)
+            pltpu.VMEM(self.shape(cut, step), BF16)
+            for slot, (_, begin, end) in enumerate(self.parts)
+            for cut in self.cuts(slot)
+            for step in range(begin, end)
         ]
-        sems = pltpu.SemaphoreType.DMA((len(self.cuts), self.steps))
+        sems = pltpu.SemaphoreType.DMA((len(lands),))
         return lands + [sems, sems]
-
-    def scratch_count(self):
-        return len(self.cuts) * self.steps + 2
 
     def bind(self, refs):
         self.refs = refs
 
-    def chunks(self, slot, source, result):
+    def chunks(self, slot, sources, results):
         send_sems, recv_sems = self.refs[-2:]
-        return [
-            [
-                Chunk(
-                    source,
-                    rows,
-                    cols,
-                    order,
-                    self.refs[item * self.steps : (item + 1) * self.steps],
-                    send_sems.at[item],
-                    recv_sems.at[item],
-                    result,
+        orders = orders_of(self.bits)
+        waves, begin, end = self.parts[slot]
+        item = sum(len(self.cuts(other)) for other in range(slot))
+        made, local = [], 0
+        for wave in waves:
+            made.append([])
+            for rows, cols, which in wave:
+                order = orders[which][0]
+                low, high = self.spans[item + local]
+                dims = [bit for bit in range(self.bits - 1, -1, -1) if bit not in order[:begin]]
+                made[-1].append(
+                    Chunk(
+                        sources[local] if isinstance(sources, (list, tuple)) else sources,
+                        rows,
+                        cols,
+                        order[begin:end],
+                        dims,
+                        self.refs[low:high],
+                        [send_sems.at[spot] for spot in range(low, high)],
+                        [recv_sems.at[spot] for spot in range(low, high)],
+                        results[local] if isinstance(results, (list, tuple)) else results,
+                    )
                 )
-                for item, rows, cols, order in wave
-            ]
-            for wave in self.waves[slot]
-        ]
+                local += 1
+        return made
+
+
+def wave_lists(bits, blocks, loads):
+    return [wave_plan(rows, width, orders_of(bits), loads) for rows, width in blocks]
 
 
 def fold(values, target):
@@ -887,15 +914,19 @@
 def decode_back_kernel(plan, bits, *refs):
     (cotangent_hbm, places_hbm, norm, *refs) = refs
     load_hbm, refs = refs[:15], refs[15:]
-    (returned, qkv_out, pos_out, embed_out, norm_sum, bias_sum, up_sum, *refs) = refs
-    (down_done, up_done, out_done, *refs) = refs
+    (returned, pos_out, embed_out, norm_sum, bias_sum, up_sum, down_done, *refs) = refs
+    handed = []
+    for slot in (1, 2, 3):
+        count = len(plan.cuts(slot))
+        handed.append(refs[:count])
+        refs = refs[count:]
     (cotangent, places, *refs) = refs
     load_vmem, refs = refs[:15], refs[15:]
     (
         active, down_w, slope, second, up_w, middle, attended, out_w, probs, packed,
         normed, placed, qkv_w, encoded, embed_w,
     ) = load_vmem
-    (down_grad, up_grad, out_grad, grad_middle, attn_grad, grad_rows, grad_keys, grad_values,
+    (down_grad, up_grad, out_grad, qkv_grad, grad_middle, attn_grad, grad_rows, grad_keys, grad_values,
      grad_packed, picked, load_sems, *refs) = refs
     plan.bind(refs)
     greet(bits)
@@ -918,7 +949,7 @@
     inner, hidden = out_w.shape[0], up_w.shape[1]
     visible = encoded.shape[0]
     blocks = length // BLOCK
-    flow = Flow(bits + 1, 2)
+    flow = Flow(2)
 
     def send(slot, source, result):
         for wave in plan.chunks(slot, source, result):
@@ -970,10 +1001,10 @@
     for item in range(4):
         cols = slice(item * panel, (item + 1) * panel)
         up_grad[:, :, :, :, :, cols] = fold(dot(second_t, slope[:, cols]), up_grad)
-    send(1, up_grad, up_done)
+    send(1, up_grad, handed[0])
     need("attended")
     out_grad[...] = fold(dot(attended[...].T, attn_grad[...]), out_grad)
-    send(2, out_grad, out_done)
+    send(2, out_grad, handed[1])
     need("probs", "packed")
     keys = packed[:, inner : 2 * inner]
     values = packed[:, 2 * inner :]
@@ -997,8 +1028,9 @@
             grad_packed[:, 2 * inner :] = value_part.astype(BF16)
         flow.tick()
     need("normed", "placed", "qkv_w", "places")
-    qkv_out[...] = fold(dot(normed[...].T, grad_packed[...]), qkv_out)
+    qkv_grad[...] = fold(dot(normed[...].T, grad_packed[...]), qkv_grad)
     flow.tick()
+    send(3, qkv_grad, handed[2])
     spots = places[:, pl.ds(0, visible)]
 
     def start_back(block, grad_normed):
@@ -1021,7 +1053,8 @@
         bias_sum[3:4, :] = fill_part
         picked[...] = pick_part
         pos_out[:, :, :, :, :, rows] = fold(rounded.T, pos_out)
-        flow.tick()
+        if block == 1:
+            flow.tick()
 
     staggered(
         range(blocks),
@@ -1037,11 +1070,16 @@
 
 
 def encode_back_kernel(plan, bits, *refs):
-    (returned, aux, norm, dec_norm_sum, dec_bias_sum, dec_up_sum, *refs) = refs
-    early, refs = refs[:3], refs[3:]
+    (sensor, returned, norm, dec_norm_sum, dec_bias_sum, dec_up_sum, *refs) = refs
+    early, refs = refs[:2], refs[2:]
+    handed = []
+    for slot in (0, 1, 2):
+        count = len(plan.cuts(slot))
+        handed.append(refs[:count])
+        refs = refs[count:]
     load_hbm, refs = refs[:13], refs[13:]
     (input_grad, small_done, *refs) = refs
-    done, refs = refs[:7], refs[7:]
+    done, refs = refs[:9], refs[9:]
     load_vmem, refs = refs[:13], refs[13:]
     (
         active, down_w, slope, second, up_w, middle, attended, out_w, probs, packed,
@@ -1063,14 +1101,14 @@
     inner, hidden = out_w.shape[0], up_w.shape[1]
     width = start.shape[1]
     greeted(bits)
-    flow = Flow(bits + 1, 2)
+    flow = Flow(2)
 
     def send(slot, source, result, part=None):
         waves = plan.chunks(slot, source, result)
         for wave in waves if part is None else waves[part : part + 1]:
             flow.add(wave)
 
-    for slot, source in enumerate(early):
+    for slot, source in enumerate([*handed, *early]):
         send(slot, source, done[slot])
     branch = returned[...]
     small[...] = jnp.zeros_like(small)
@@ -1082,7 +1120,7 @@
         target = down_grad.at[item // 2, item % 2]
         target[...] = dot(active[:, cols].T, branch).astype(BF16).reshape(target.shape)
     flow.tick()
-    send(3, down_grad, done[3], 0)
+    send(5, down_grad, done[5], 0)
     need("second", "slope", "down_w")
     second_t = second[...].T
     for item in range(4):
@@ -1091,8 +1129,9 @@
         slope[:, cols] = lifted_back
         small[10 + item : 11 + item, :] = column_sum(lifted_back.astype(F32))
         up_grad[:, :, :, :, :, cols] = fold(dot(second_t, lifted_back), up_grad)
-    flow.tick()
-    send(3, down_grad, done[3], 1)
+        if item % 2:
+            flow.tick()
+    send(5, down_grad, done[5], 1)
     need("up_w", "middle", "out_w", "attended")
     grad_second = dot_nt(slope[...], up_w[...])
     inward, small[2:3, :], small[3:4, :] = norm_back(grad_second, middle[...], row(norm, 2))
@@ -1100,11 +1139,11 @@
     attn_grad = grad_middle.astype(BF16)
     small[4:5, :] = column_sum(attn_grad.astype(F32))
     flow.tick()
-    send(4, up_grad, done[4], 0)
+    send(6, up_grad, done[6], 0)
     out_grad[...] = fold(dot(attended[...].T, attn_grad), out_grad)
     grad_rows = dot_nt(attn_grad, out_w[...]).astype(BF16)
     flow.tick()
-    send(4, up_grad, done[4], 1)
+    send(6, up_grad, done[6], 1)
     need("probs", "packed")
     scale = HEAD_DIM**-0.5
     heads = LANES // HEAD_DIM
@@ -1126,18 +1165,20 @@
         grad_packed[:, 2 * inner + base : 2 * inner + base + LANES] = value_part.astype(BF16)
     flow.tick()
     need("normed", "start", "qkv_w")
-    send(5, out_grad, done[5])
+    send(7, out_grad, done[7])
     normed_t = normed[...].T
     for item in range(3):
         cols = slice(item * inner, (item + 1) * inner)
         qkv_grad[:, :, :, :, :, cols] = fold(dot(normed_t, grad_packed[:, cols]), qkv_grad)
     flow.tick()
-    send(6, qkv_grad, done[6])
+    send(8, qkv_grad, done[8])
     grad_normed = dot_nt(grad_packed[...], qkv_w[...])
     inward, small[0:1, :], small[1:2, :] = norm_back(grad_normed, start[...], row(norm, 0))
     grad_start = grad_middle + inward
     input_grad[...] = grad_start
-    small[6:10, :] = aux[4:8, : start.shape[1]] * column_sum(grad_start)
+    kinds = lax.broadcasted_iota(jnp.int32, (4, width), 0)
+    mine = kinds == sensor[lax.axis_index("section")]
+    small[6:10, :] = jnp.where(mine, column_sum(grad_start), 0.0)
     dec_width = dec_norm_sum.shape[1]
     small[14:18, :dec_width] = dec_norm_sum[...]
     small[18:22, :dec_width] = dec_bias_sum[...]
@@ -1224,17 +1265,21 @@
         active, down_w, slope, second, up_w, middle, attended, out_w, probs, packed, normed,
         placed, qkv_w, encoded, embed_w,
     ]
-    sent = [blocked(*item.shape, bits) for item in (down_w, up_w, out_w)]
-    plan = Plan(bits, [(item[-2], item[-1] // 2) for item in sent])
-    later = [blocked(*qkv_w.shape, bits), blocked(width, length, bits), blocked(*embed_w.shape, bits)]
-    return pl.pallas_call(
+    sent = [blocked(*item.shape, bits) for item in (down_w, up_w, out_w, qkv_w)]
+    later = [blocked(width, length, bits), blocked(*embed_w.shape, bits)]
+    waves = wave_lists(bits, [(item[-2], item[-1] // 2) for item in sent], [0.0, 0.0, 0.0])
+    ends = (bits + 1, 2, 2, 1)
+    plan = Plan(bits, [(wave, 0, end) for wave, end in zip(waves, ends)])
+    handed = [plan.handed(slot) for slot in (1, 2, 3)]
+    results = pl.pallas_call(
         partial(decode_back_kernel, plan, bits),
         out_shape=[shaped(encoded.shape, BF16)]
         + [shaped(item, BF16) for item in later]
         + [shaped((4, width), F32), shaped((4, width), F32), shaped((1, hidden), F32)]
-        + [shaped((item[-2], item[-1] // 2), F32) for item in sent],
+        + [shaped((sent[0][-2], sent[0][-1] // 2), F32)]
+        + [shaped(item, BF16) for group in handed for item in group],
         in_specs=[APART, APART, WHOLE] + [APART] * len(loaded),
-        out_specs=[WHOLE] * 10,
+        out_specs=[WHOLE] * (7 + sum(len(group) for group in handed)),
         scratch_shapes=[
             pltpu.VMEM((length, width), BF16),
             pltpu.VMEM((1, length), jnp.int32),
@@ -1255,9 +1300,14 @@
         compiler_params=communicating(1),
         name="decode_back",
     )(cotangent, order, norm, *loaded)
-
-
-def run_encode_back(returned, aux, stored, enc_w, early, dec_sums, bits):
+    rest = results[7:]
+    parts = [
+        (waves[slot], ends[slot], (sent[slot][-2], sent[slot][-1] // 2)) for slot in (1, 2, 3)
+    ]
+    return results[0], results[1:3], results[3:6], results[6], rest, parts
+
+
+def run_encode_back(returned, sensor, stored, enc_w, early, dec_sums, handed, parts, bits):
     norm, qkv_w, out_w, bias, up_w, up_bias, down_w, table = enc_w
     start, normed, packed, probs, attended, middle, second, active, slope = stored
     shaped = jax.ShapeDtypeStruct
@@ -1266,16 +1316,23 @@
         start, qkv_w,
     ]
     own = [blocked(*item.shape, bits) for item in (down_w, up_w, out_w, qkv_w)]
-    sent = [item.shape for item in early] + own
-    plan = Plan(bits, [(item[-2], item[-1] // 2) for item in sent])
+    whole = [item.shape for item in early] + own
+    blocks = [(item[-2], item[-1] // 2) for item in whole]
+    waves = wave_lists(bits, blocks, [0.0, 0.0, 0.0])
+    plan = Plan(
+        bits,
+        [(wave, begin, bits + 1) for wave, begin, _ in parts]
+        + [(wave, 0, bits + 1) for wave in waves],
+    )
+    blocks = [block for _, _, block in parts] + blocks
     width = start.shape[1]
     small = (SMALL_ROWS, width)
     return pl.pallas_call(
         partial(encode_back_kernel, plan, bits),
         out_shape=[shaped(start.shape, F32), shaped(small, F32)]
-        + [shaped((item[-2], item[-1] // 2), F32) for item in sent],
-        in_specs=[WHOLE] * 9 + [APART] * len(loaded),
-        out_specs=[WHOLE] * 9,
+        + [shaped(block, F32) for block in blocks],
+        in_specs=[SCALARS] + [WHOLE] * (7 + len(handed)) + [APART] * len(loaded),
+        out_specs=[WHOLE] * 11,
         scratch_shapes=[like(item) for item in loaded]
         + [pltpu.VMEM(item, BF16) for item in own]
         + [
@@ -1289,7 +1346,7 @@
         + plan.scratch(),
         compiler_params=communicating(2),
         name="encode_back",
-    )(returned, aux, norm, *dec_sums, *early, *loaded)
+    )(sensor, returned, norm, *dec_sums, *early, *handed, *loaded)
 
 
 def local_rows(whole, shape):
@@ -1346,30 +1403,15 @@
     if not fits:
         return plain_shards(tokens, order, sensor, cotangent, enc_w, dec_w)
     bits = datas.bit_length() - 1
-    kind = lax.dynamic_index_in_dim(sensor, lax.axis_index("section"), 0, keepdims=False)
-    kinds = (jnp.arange(enc_w[7].shape[0]) == kind).astype(F32)[:, None]
-    hidden = enc_w[4].shape[1]
-
-    def wide(item):
-        return jnp.pad(item, ((0, 0), (0, hidden - item.shape[1])))
-
-    aux = jnp.concatenate(
-        [
-            enc_w[5].astype(F32)[None],
-            wide(dec_w[6].astype(F32)[None]),
-            wide(jnp.sum(kinds * enc_w[7].astype(F32), axis=0, keepdims=True)),
-            jnp.zeros((1, hidden), F32),
-            jnp.broadcast_to(kinds, (kinds.shape[0], hidden)),
-        ]
-    )
-    enc_kept, encoded, decoded, dec_kept = run_forward(tokens, order, aux, enc_w, dec_w)
-    back = run_decode_back(cotangent, order, dec_kept, encoded, dec_w, bits)
-    returned, early, dec_sums, dec_done = back[0], back[1:4], back[4:7], back[7:]
-    down_dec, up_dec, out_dec = dec_done
+    kinds = sensor.reshape(-1)
+    enc_kept, encoded, decoded, dec_kept = run_forward(tokens, order, kinds, enc_w, dec_w)
+    returned, early, dec_sums, down_dec, handed, parts = run_decode_back(
+        cotangent, order, dec_kept, encoded, dec_w, bits
+    )
     input_grad, small, *rest = run_encode_back(
-        returned, aux, enc_kept, enc_w, early, dec_sums, bits
-    )
-    qkv_dec, pos, embed, down, up, out, qkv = rest
+        returned, kinds, enc_kept, enc_w, early, dec_sums, handed, parts, bits
+    )
+    up_dec, out_dec, qkv_dec, pos, embed, down, up, out, qkv = rest
     tiny_slots = (0, 3, 7, 5, 9, 12, 14)
     shapes = [
         (item.shape[0] // 2, item.shape[1] // datas)

time: 186 us -> 178 us (0.957)
  Pallas kernels: 178 us -> 175 us
  local copies, waits for them, and re-layouts: 2.76 us -> 0 us
  other arithmetic: 2.13 us -> 0 us
    pallas_call x1, Pallas kernels: 47.1 us -> 40.7 us  [run_decode_back(): pl.pallas_call(partial(decode_back_kernel, plan, bits), out_shape=[shaped...]
    pallas_call x1, Pallas kernels: 81.1 us -> 84.7 us  [run_encode_back(): pl.pallas_call(partial(encode_back_kernel, plan, bits), out_shape=[shaped...]
where the time goes in v1:
time: 178 us; the launch traced here: 176 us
  Pallas kernels  175 us (98%)
    pallas_call x1, Pallas kernels, run_encode_back(): pl.pallas_call(partial(encode_back_kernel, plan, bits), out_shape=[shaped...  84.7 us
    pallas_call x1, Pallas kernels, run_forward(): pl.pallas_call(forward_kernel, out_shape=enc_kept + [shaped((length, dec_...  46 us
    pallas_call x1, Pallas kernels, run_decode_back(): pl.pallas_call(partial(decode_back_kernel, plan, bits), out_shape=[shaped...  40.7 us
    pallas_call x1, Pallas kernels, run_finish(): pl.pallas_call(partial(finish_kernel, (len(shapes), len(big))), out_shape...  3.89 us

profile of v1, /device:TPU:0, one launch (start us, length us, event | category | flops | bytes accessed | tf_op | source)
XLA Modules:
  0.0 176.2 jit_solution(15374367274380417624)
XLA Ops:
  0.7 46.0 %forward.1 = (f32[256,768]{1,0:T(8,128)}, bf16[256,768]{1,0:T(8,128)(2,1)}, bf16[256,2304]{1,0:T(8,128)(2,1)}, bf16[12,256,256]{2,1,0:T(8,128)(2,1)}, bf16[256,7...) custom-call(s32[2]{0:T(128)} %bitcast.6, ...), custom_call_target="tpu_custom_call" | custom-call | tf_op jit(solution)/shard_map/forward/pallas_call | solution.py:767
  46.7 40.7 %decode_back.1 = (bf16[256,768]{1,0:T(8,128)(2,1)}, bf16[2,2,2,2,32,1024]{5,4,3,2,1,0:T(8,128)(2,1)}, bf16[2,2,2,2,48,512]{5,4,3,2,1,0:T(8,128)(2,1)}, f32[4,512...) custom-call(bf16[2,1,1024,512]{3,2,1,0:T(8,128)(2,1)} %refs_0_.1, ...), custom_call_target="tpu_custom_call" | custom-call | tf_op jit(solution)/shard_map/decode_back/pallas_call | solution.py:1274
  87.4 84.7 %encode_back.1 = (f32[256,768]{1,0:T(8,128)}, f32[32,768]{1,0:T(8,128)}, f32[32,1024]{1,0:T(8,128)}, f32[16,256]{1,0:T(8,128)}, f32[32,384]{1,0:T(8,128)}, /*ind...) custom-call(s32[2]{0:T(128)} %bitcast.7, ...), custom_call_target="tpu_custom_call" | custom-call | tf_op jit(solution)/shard_map/encode_back/pallas_call | solution.py:1330
  172.1 3.9 %finish.1 = (f32[2,48]{1,0:T(2,128)}, f32[1,48]{1,0:T(1,128)}, f32[2,48]{1,0:T(2,128)}, f32[1,96]{1,0:T(1,128)}, f32[2,32]{1,0:T(2,128)}, /*index=5*/f32[2,32]{1...) custom-call(f32[32,768]{1,0:T(8,128)} %get-tuple-element.117.refs_0_, ...), custom_call_target="tpu_custom_call" | custom-call | tf_op jit(solution)/shard_map/finish/pallas_call | solution.py:1237
